TPU v7x, 32 devices: a whole 2x2x4 slice. The times are simulated.
32 devices in a mesh: grp: 2 (over core), req: 16 (over z, y, x).
Axes of the slice: x: 2, y: 2, z: 4, core: 2. Of those that a mesh axis runs over, the one named last changes fastest.
Arguments:
- new_qkv: bfloat16 [128, 32, 3840], P(('grp', 'req')), parts along dimension 0, may hold values from -5 to 5
- cache_kv: bfloat16 [128, 32, 2560], P(('grp', 'req')), parts along dimension 0, may hold values from -5 to 5
- resid: bfloat16 [128, 32, 1280], P(('grp', 'req')), parts along dimension 0, may hold values from -6 to 6
- span_len: int32 [128], P(('grp', 'req')), parts along dimension 0, may hold values from 1 to 32
- cache_len: int32 [128], P(('grp', 'req')), parts along dimension 0, may hold values from 0 to 32
- series_perm: int32 [128], P(('grp', 'req')), parts along dimension 0, may hold values from 0 to 63, each once
- ff_gain: float32 [1280], replicated, may hold values from 0.5 to 1.5
- w_up: bfloat16 [1280, 1280], replicated, may hold values from -0.15625 to 0.15625
- w_down: bfloat16 [1280, 1280], replicated, may hold values from -0.15625 to 0.15625
Outputs:
- packed_out: bfloat16 [4096, 1280], P(('grp', 'req')), parts along dimension 0
There are 2 independent parts, one for each index of `grp`. A program takes and returns all parts, laid end to end along the dimension named above; an argument that names none is the same for every part. Nothing has to cross between parts.
Inputs may be any that keep to these rules, and one draw needn't show every extreme that they name: `series_perm`: each series id appears once.
All inputs are finite; a program needn't handle non-finite values.
Results may differ from a plain program's by a relative error of at most 0.0055.
Values may be sent and summed in bfloat16 or wider, within the bound.
A program may use at most 64 MiB of HBM per device.

v0:
```python
import functools

import jax
import jax.numpy as jnp
from jax import lax
from jax.experimental import pallas as pl
from jax.experimental.pallas import tpu as pltpu
from jax.sharding import PartitionSpec as P

H = 16
LANES = 128
ROWS = 8
CUTS = (1280,)


def div(x, k):
    return lax.shift_right_arithmetic(x, jnp.int32(k.bit_length() - 1)) if k & (k - 1) == 0 else x // k


def mod(x, k):
    return x & (k - 1) if k & (k - 1) == 0 else x % k


def windows(heads, head_size):
    found = []
    for h in heads:
        if found and (h + 1) * head_size <= found[-1][0] + 2 * LANES:
            found[-1][1].append(h)
        else:
            found.append((h * head_size // LANES * LANES, [h]))
    return found


def kernel(
    n, series, span, cache, width,
    qkv_hbm, cache_hbm, resid_hbm, len_hbm, clen_hbm, perm_hbm, gain_hbm, up_hbm, down_hbm,
    out_ref,
    qkv, ckv, resid, len_ref, clen_ref, perm_ref, gain, w_up, w_down, hid, act, meta_send, meta, sends, recvs,
    load_sem, meta_ssem, meta_rsem, ssems, rsems,
):
    me = lax.axis_index("req")
    head_size = width // H
    per = (span + n - 1) // n
    rows_here = series * span
    tiles = n * ROWS // LANES
    group = LANES // ROWS

    loads = [
        pltpu.make_async_copy(src, dst, load_sem.at[k])
        for k, (src, dst) in enumerate(
            (
                (len_hbm, len_ref), (perm_hbm, perm_ref), (clen_hbm, clen_ref), (qkv_hbm, qkv), (cache_hbm, ckv),
                (resid_hbm, resid), (gain_hbm, gain), (up_hbm, w_up), (down_hbm, w_down),
            )
        )
    ]
    barrier = pltpu.get_barrier_semaphore()

    @pl.loop(1, n, unroll=n <= 16)
    def _(k):
        pl.semaphore_signal(
            barrier, inc=1, device_id={"req": lax.rem(me + k, n)}, device_id_type=pl.DeviceIdType.MESH
        )

    for load in loads:
        load.start()
    for load in loads[:2]:
        load.wait()

    sub = lax.broadcasted_iota(jnp.int32, (ROWS, LANES), 0)
    lens = jnp.zeros((ROWS, LANES), jnp.int32)
    ids = jnp.zeros((ROWS, LANES), jnp.int32)
    for i in range(series):
        lens = jnp.where(sub == i, len_ref[i], lens)
        ids = jnp.where(sub == i, perm_ref[i], ids)
    meta_send[0:ROWS] = lens
    meta_send[ROWS:] = ids
    meta[me] = meta_send[...]

    def meta_copy(peer, slot):
        return pltpu.make_async_remote_copy(
            src_ref=meta_send, dst_ref=meta.at[slot], send_sem=meta_ssem.at[peer], recv_sem=meta_rsem.at[slot],
            device_id={"req": peer}, device_id_type=pl.DeviceIdType.MESH,
        )

    for load in loads[2:6]:
        load.wait()

    lane = lax.broadcasted_iota(jnp.int32, (1, 2 * LANES), 1)
    key_pos = lax.broadcasted_iota(jnp.int32, (span, cache + span), 1)
    row_pos = lax.broadcasted_iota(jnp.int32, (span, cache + span), 0)

    def attend(heads):
        wins = windows(heads, head_size)
        first, last = heads[0] * head_size, (heads[-1] + 1) * head_size

        @pl.loop(0, series, unroll=2)
        def _(i):
            limit = clen_ref[i]
            visible = (key_pos < limit) | ((key_pos >= cache) & (key_pos - cache <= row_pos))
            parts = {}
            for base, group_heads in wins:
                wide = min(2 * LANES, width - base)
                masks = [
                    jnp.where(
                        (lane[:, :wide] >= h * head_size - base) & (lane[:, :wide] < (h + 1) * head_size - base),
                        1.0, 0.0,
                    )
                    for h in group_heads
                ]
                q = qkv[i, :, base : base + wide]
                qs = jnp.concatenate([q * m.astype(jnp.bfloat16) for m in masks], axis=0)
                keys = jnp.concatenate(
                    [ckv[i, :, base : base + wide], qkv[i, :, width + base : width + base + wide]], axis=0
                )
                values = jnp.concatenate(
                    [ckv[i, :, width + base : width + base + wide],
                     qkv[i, :, 2 * width + base : 2 * width + base + wide]], axis=0
                )
                s = lax.dot_general(qs, keys, (((1,), (1,)), ((), ())), preferred_element_type=jnp.float32)
                s = s.reshape(len(masks), span, cache + span) * head_size ** (-0.5)
                s = jnp.where(visible[None], s, -1e30)
                e = jnp.exp(s - jnp.max(s, axis=-1, keepdims=True))
                w = (e * (1.0 / jnp.sum(e, axis=-1, keepdims=True))).astype(jnp.bfloat16)
                o = jnp.dot(
                    w.reshape(len(masks) * span, cache + span), values, preferred_element_type=jnp.float32
                )
                total = sum(o[k * span : (k + 1) * span] * m for k, m in enumerate(masks))
                for at in range(0, wide, LANES):
                    piece = total[:, at : at + LANES]
                    parts[base + at] = parts[base + at] + piece if base + at in parts else piece
            for at, piece in parts.items():
                if first <= at and at + LANES <= last:
                    hid[pl.ds(pl.multiple_of(i * span, span), span), at : at + LANES] = (
                        resid[i, :, at : at + LANES].astype(jnp.float32) + piece
                    ).astype(jnp.bfloat16)

    lane1 = lax.broadcasted_iota(jnp.int32, (1, LANES), 1)

    def starts_of(ids_of_lanes):
        earlier = jnp.where(meta[:, ROWS:, :] < ids_of_lanes[None], meta[:, :ROWS, :], 0)
        return jnp.sum(jnp.sum(earlier, axis=0), axis=0, keepdims=True)

    def block_copy(c, peer, slot):
        return pltpu.make_async_remote_copy(
            src_ref=sends[c].at[peer], dst_ref=recvs[c].at[slot], send_sem=ssems.at[c, peer],
            recv_sem=rsems.at[c, slot], device_id={"req": peer}, device_id_type=pl.DeviceIdType.MESH,
        )

    pl.semaphore_wait(barrier, n - 1)

    @pl.loop(1, n, unroll=n <= 16)
    def _(k):
        meta_copy(lax.rem(me + k, n), me).start()

    attend(list(range(H)))
    loads[6].wait()
    hidden = hid[...].astype(jnp.float32)
    normed = (
        hidden * lax.rsqrt(jnp.mean(hidden * hidden, axis=-1, keepdims=True) + 1e-06) * gain[...].reshape(1, width)
    ).astype(jnp.bfloat16)
    loads[7].wait()
    step = 256
    for at in range(0, w_up.shape[1], step):
        v = jnp.dot(normed, w_up[:, at : at + step], preferred_element_type=jnp.float32)
        act[:, at : at + step] = (v * (1.0 / (1.0 + jnp.exp(-v)))).astype(jnp.bfloat16)
    loads[8].wait()
    for at in range(0, width, step):
        v = jnp.dot(act[...], w_down[:, at : at + step], preferred_element_type=jnp.float32)
        hid[:, at : at + step] = (hid[:, at : at + step].astype(jnp.float32) + v).astype(jnp.bfloat16)

    place = None
    done = 0
    for c, cut in enumerate(CUTS):
        if c == 0:
            @pl.loop(1, n, unroll=n <= 16)
            def _(k):
                src = lax.rem(me + n - k, n)
                meta_copy(src, src).wait_recv()

            own_ids = jnp.zeros((1, rows_here), jnp.int32)
            own_len = jnp.zeros((1, rows_here), jnp.int32)
            token = lax.broadcasted_iota(jnp.int32, (1, rows_here), 1)
            own = div(token, span)
            slot = mod(token, span)
            for i in range(series):
                own_ids = jnp.where(own == i, perm_ref[i], own_ids)
                own_len = jnp.where(own == i, len_ref[i], own_len)
            at = mod(starts_of(own_ids) + slot, n) * ROWS + own * per + div(slot, n)
            place = jnp.where(slot < own_len, at, -1)
        half = (cut - done) // 2
        rows = lax.broadcasted_iota(jnp.int32, (LANES, rows_here), 0)
        for k in range(tiles):
            pick = jnp.where(rows + k * LANES == place, 1.0, 0.0).astype(jnp.bfloat16)
            moved = jnp.dot(pick, hid[:, done:cut], preferred_element_type=jnp.float32)
            moved = jnp.concatenate(
                [moved[:, :half].reshape(group, ROWS, half), moved[:, half:].reshape(group, ROWS, half)], axis=1
            )
            sends[c][k * group : (k + 1) * group] = moved.astype(jnp.bfloat16)

        @pl.loop(1, n, unroll=n <= 16)
        def _(k, c=c):
            block_copy(c, lax.rem(me + k, n), me).start()

        recvs[c][me] = sends[c][me]
        done = cut

    sub = lax.broadcasted_iota(jnp.int32, (ROWS, LANES), 0)
    lane8 = lax.broadcasted_iota(jnp.int32, (ROWS, LANES), 1)
    local = []
    for k in range(tiles):
        a_ids = jnp.zeros((ROWS, LANES), jnp.int32)
        a_len = jnp.zeros((ROWS, LANES), jnp.int32)
        for s in range(group):
            mine = (div(lane8, ROWS) == s) & (div(mod(lane8, ROWS), per) == sub)
            a_ids = jnp.where(mine, meta[k * group + s, ROWS:, :], a_ids)
            a_len = jnp.where(mine, meta[k * group + s, :ROWS, :], a_len)
        a_ids = jnp.sum(a_ids, axis=0, keepdims=True)
        a_len = jnp.sum(a_len, axis=0, keepdims=True)
        begin = starts_of(a_ids)
        t = mod(me - begin, n) + n * mod(lane1, per)
        local.append(jnp.where(t < a_len, div(begin + t, n), -1))

    out_rows = lax.broadcasted_iota(jnp.int32, (rows_here, LANES), 0)
    picks = [jnp.where(out_rows == spot, 1.0, 0.0).astype(jnp.bfloat16) for spot in local]
    for c in range(len(CUTS)):
        @pl.loop(1, n, unroll=n <= 16)
        def _(k, c=c):
            src = lax.rem(me + n - k, n)
            block_copy(c, src, src).wait_recv()

        total = None
        for k in range(tiles):
            got = recvs[c][k * group : (k + 1) * group].astype(jnp.float32)
            half = got.shape[2]
            got = jnp.concatenate(
                [got[:, :ROWS].reshape(LANES, half), got[:, ROWS:].reshape(LANES, half)], axis=1
            ).astype(jnp.bfloat16)
            more = jnp.dot(picks[k], got, preferred_element_type=jnp.float32)
            total = more if total is None else total + more
        out_ref[:, (CUTS[c - 1] if c else 0) : CUTS[c]] = total.astype(jnp.bfloat16)

    @pl.loop(1, n, unroll=n <= 16)
    def _(k):
        peer = lax.rem(me + k, n)
        meta_copy(peer, me).wait_send()
        for c in range(len(CUTS)):
            block_copy(c, peer, me).wait_send()


def local(new_qkv, cache_kv, resid, span_len, cache_len, series_perm, ff_gain, w_up, w_down):
    n = lax.axis_size("req")
    series, span, _ = new_qkv.shape
    cache, width, hidden = cache_kv.shape[1], resid.shape[2], w_up.shape[1]
    rows_here = series * span
    halves = [(b - a) // 2 for a, b in zip((0,) + CUTS, CUTS)]
    hbm, vmem = (pl.BlockSpec(memory_space=m) for m in (pltpu.HBM, pltpu.VMEM))
    return pl.pallas_call(
        functools.partial(kernel, n, series, span, cache, width),
        out_shape=jax.ShapeDtypeStruct((rows_here, width), jnp.bfloat16),
        in_specs=[hbm] * 9,
        out_specs=vmem,
        scratch_shapes=[
            pltpu.VMEM(new_qkv.shape, jnp.bfloat16),
            pltpu.VMEM(cache_kv.shape, jnp.bfloat16),
            pltpu.VMEM(resid.shape, jnp.bfloat16),
            pltpu.SMEM(span_len.shape, jnp.int32),
            pltpu.SMEM(cache_len.shape, jnp.int32),
            pltpu.SMEM(series_perm.shape, jnp.int32),
            pltpu.VMEM(ff_gain.shape, jnp.float32),
            pltpu.VMEM(w_up.shape, jnp.bfloat16),
            pltpu.VMEM(w_down.shape, jnp.bfloat16),
            pltpu.VMEM((rows_here, width), jnp.bfloat16),
            pltpu.VMEM((rows_here, hidden), jnp.bfloat16),
            pltpu.VMEM((2 * ROWS, LANES), jnp.int32),
            pltpu.VMEM((n, 2 * ROWS, LANES), jnp.int32),
            [pltpu.VMEM((n, 2 * ROWS, h), jnp.bfloat16) for h in halves],
            [pltpu.VMEM((n, 2 * ROWS, h), jnp.bfloat16) for h in halves],
            pltpu.SemaphoreType.DMA((9,)),
            pltpu.SemaphoreType.DMA((n,)),
            pltpu.SemaphoreType.DMA((n,)),
            pltpu.SemaphoreType.DMA((len(CUTS), n)),
            pltpu.SemaphoreType.DMA((len(CUTS), n)),
        ],
        compiler_params=pltpu.CompilerParams(
            collective_id=0, has_side_effects=True, vmem_limit_bytes=64 * 2**20
        ),
    )(new_qkv, cache_kv, resid, span_len, cache_len, series_perm, ff_gain, w_up, w_down)


def solution(mesh):
    rows3, rows1 = P(("grp", "req"), None, None), P(("grp", "req"))
    in_specs = (rows3, rows3, rows3, rows1, rows1, rows1, P(), P(), P())
    out_specs = P(("grp", "req"), None)
    return jax.shard_map(local, mesh=mesh, in_specs=in_specs, out_specs=out_specs, check_vma=False)
```

profile of v0, /device:TPU:15, one launch (start us, length us, event | category | flops | bytes accessed | tf_op | source)
XLA Modules:
  0.0 22.3 jit_solution(5824842411367821421)
XLA Ops:
  0.0 20.6 %shard_map.91 = bf16[128,1280]{1,0:T(8,128)(2,1)} custom-call(bf16[4,32,3840]{2,1,0:T(8,128)(2,1)} %qkv_hbm.1, bf16[4,32,2560]{2,1,0:T(8,128)(2,1)} %cache_hbm.1, bf16[4,32,1280]{2,1,0:T(8,128)(2,1)} %resid_hbm.1, s32[4]{0:T(128)} %len_hbm.1, s32[4]{0:T(128)} %clen_hbm.1, s32[4]{0:T(128)} %perm_hbm.1, f32[1280]{0:T(1024)} %gain_hbm.1, ...), custom_call_target="tpu_custom_call" | custom-call | tf_op jit(solution)/shard_map/pallas_call | solution.py:258
  20.6 1.7 %copy.11 = bf16[128,1280]{1,0:T(8,128)(2,1)} copy(bf16[128,1280]{1,0:T(8,128)(2,1)} %shard_map.91) | data formatting | bytes 655360
where the time goes:
time: 22.5 us; the launch traced here: 22.3 us
  Pallas kernels  20.6 us (92%)
  local copies, waits for them, and re-layouts  1.72 us (8%)
    pallas_call x1, Pallas kernels, local(): pl.pallas_call(functools.partial(kernel, n, series, span, cache, width),...  20.6 us
    unnamed x1, local copies, waits for them, and re-layouts  1.72 us

commit v1 on v0

--- a/solution.py
+++ b/solution.py
@@ -94,7 +94,7 @@
         wins = windows(heads, head_size)
         first, last = heads[0] * head_size, (heads[-1] + 1) * head_size
 
-        @pl.loop(0, series, unroll=2)
+        @pl.loop(0, series, unroll=True)
         def _(i):
             limit = clen_ref[i]
             visible = (key_pos < limit) | ((key_pos >= cache) & (key_pos - cache <= row_pos))

time: 22.5 us -> 21.8 us (0.969)
  Pallas kernels: 20.6 us -> 19.9 us
    pallas_call x1, Pallas kernels: 20.6 us -> 19.9 us  [local(): pl.pallas_call(functools.partial(kernel, n, series, span, cache, width),...]
where the time goes in v1:
time: 21.8 us; the launch traced here: 21.7 us
  Pallas kernels  19.9 us (91%)
  local copies, waits for them, and re-layouts  1.72 us (8%)
    pallas_call x1, Pallas kernels, local(): pl.pallas_call(functools.partial(kernel, n, series, span, cache, width),...  19.9 us
    unnamed x1, local copies, waits for them, and re-layouts  1.72 us

profile of v1, /device:TPU:15, one launch (start us, length us, event | category | flops | bytes accessed | tf_op | source)
XLA Modules:
  0.0 21.7 jit_solution(14224317288054910254)
XLA Ops:
  0.0 19.9 %shard_map.91 = bf16[128,1280]{1,0:T(8,128)(2,1)} custom-call(bf16[4,32,3840]{2,1,0:T(8,128)(2,1)} %qkv_hbm.1, bf16[4,32,2560]{2,1,0:T(8,128)(2,1)} %cache_hbm.1, bf16[4,32,1280]{2,1,0:T(8,128)(2,1)} %resid_hbm.1, s32[4]{0:T(128)} %len_hbm.1, s32[4]{0:T(128)} %clen_hbm.1, s32[4]{0:T(128)} %perm_hbm.1, f32[1280]{0:T(1024)} %gain_hbm.1, ...), custom_call_target="tpu_custom_call" | custom-call | tf_op jit(solution)/shard_map/pallas_call | solution.py:258
  19.9 1.7 %copy.11 = bf16[128,1280]{1,0:T(8,128)(2,1)} copy(bf16[128,1280]{1,0:T(8,128)(2,1)} %shard_map.91) | data formatting | bytes 655360
